TPU v7x, 32 devices: a whole 2x2x4 slice. The times are simulated.
32 devices in a mesh: span: 16 (over z, x, core), row: 2 (over y).
Axes of the slice: x: 2, y: 2, z: 4, core: 2. Of those that a mesh axis runs over, the one named last changes fastest.
Arguments:
- features: bfloat16 [16, 4, 16, 32, 128], P('span', None, 'row'), may hold values from -6 to 6
- clip_lengths: int32 [4], replicated, may hold values from 1 to 8, 16 in all
- clip_order: int32 [4], replicated, may hold values from 0 to 3, each once
- weight_a: bfloat16 [3, 3, 3, 128, 128], replicated, may hold values from -0.109375 to 0.109375
- bias_a: float32 [128], replicated, may hold values from -3 to 3
- weight_b: bfloat16 [3, 3, 3, 128, 128], replicated, may hold values from -0.109375 to 0.109375
- bias_b: float32 [128], replicated, may hold values from -3 to 3
- weight_down: bfloat16 [3, 3, 3, 128, 128], replicated, may hold values from -0.109375 to 0.109375
- bias_down: float32 [128], replicated, may hold values from -3 to 3
Outputs:
- patch_tokens: bfloat16 [16, 2, 4, 8, 512], P('span', None, 'row')
Inputs may be any that keep to these rules, and one draw needn't show every extreme that they name: `clip_lengths`: the lengths sum to 16. `clip_order`: each clip appears once.
All inputs are finite; a program needn't handle non-finite values.
Results may differ from a plain program's by a relative error of at most 0.0051.
Values may be sent and summed in bfloat16 or wider, within the bound.
A program may use at most 64 MiB of HBM per device.

v0:
```python
import functools

import jax
import jax.numpy as jnp
from jax import lax
from jax.experimental import pallas as pl
from jax.experimental.pallas import tpu as pltpu
from jax.sharding import PartitionSpec as P

MESH = pl.DeviceIdType.MESH
UP = 3
LOW = 2
BF16 = jnp.bfloat16
F32 = jnp.float32


def kernel(
    spans,
    rows_n,
    x_hbm,
    lengths_hbm,
    order_hbm,
    wa_hbm,
    ba_hbm,
    wb_hbm,
    bb_hbm,
    wd_hbm,
    bd_hbm,
    out,
    xs,
    hs,
    ms,
    wa,
    wb,
    wd,
    ba,
    bb,
    bd,
    lengths,
    order,
    cells,
    share,
    passed,
    send_sem,
    recv_sem,
    load_sem,
):
    s = lax.axis_index("span")
    r = lax.axis_index("row")
    height, cols, chans = x_hbm.shape[2], x_hbm.shape[3], x_hbm.shape[4]
    hid_rows = height + UP
    mix_rows = height + 1
    inner = UP + height - 2

    first_s, last_s = s == 0, s == spans - 1
    first_r, last_r = r == 0, r == rows_n - 1
    no = jnp.logical_not
    both = jnp.logical_and
    s_to, r_to, r_back = (
        jnp.minimum(s + 1, spans - 1),
        jnp.minimum(r + 1, rows_n - 1),
        jnp.maximum(r - 1, 0),
    )
    s_from = jnp.maximum(s - 1, 0)
    kinds = [
        ((s, r_to), no(last_r), no(first_r), (s, r_back)),
        ((s, r_back), no(first_r), no(last_r), (s, r_to)),
        ((s_to, r), no(last_s), no(first_s), (s_from, r)),
        (
            (s_to, r_to),
            both(no(last_s), no(last_r)),
            both(no(first_s), no(first_r)),
            (s_from, r_back),
        ),
        (
            (s_to, r_back),
            both(no(last_s), no(first_r)),
            both(no(first_s), no(last_r)),
            (s_from, r_to),
        ),
    ]

    barrier = pltpu.get_barrier_semaphore()
    for _, _, receives, sender in kinds:

        @pl.when(receives)
        def _():
            pl.semaphore_signal(barrier, inc=1, device_id=sender, device_id_type=MESH)

    used = [0]

    def load(source, target):
        copy = pltpu.make_async_copy(source, target, load_sem.at[used[0]])
        used[0] += 1
        copy.start()
        return copy

    def paired(source, target):
        return [
            load(source.at[t], target.at[t + o, :, :, :, o * chans : (o + 1) * chans])
            for t in range(3)
            for o in range(2)
        ]

    load_x = [load(x_hbm.at[0], xs.at[2:6, UP : UP + height])]
    load_a = paired(wa_hbm, wa) + [load(ba_hbm, ba)]
    load_i = [load(lengths_hbm, lengths), load(order_hbm, order)]

    def blank(target):
        zeros = jnp.zeros((3, 3, chans, chans), BF16)
        target[0, :, :, :, chans : 2 * chans] = zeros
        target[3, :, :, :, 0:chans] = zeros

    blank(wa)

    greeted = sum(sends.astype(jnp.int32) for _, sends, _, _ in kinds)
    pl.semaphore_wait(barrier, greeted)

    feats = x_hbm.at[0]
    routes = [
        (feats.at[:, height - UP : height], xs.at[2:6, 0:UP]),
        (feats.at[:, 0:LOW], xs.at[2:6, UP + height : UP + height + LOW]),
        (feats.at[2:4], xs.at[0:2, UP : UP + height]),
        (feats.at[2:4, height - UP : height], xs.at[0:2, 0:UP]),
        (feats.at[2:4, 0:LOW], xs.at[0:2, UP + height : UP + height + LOW]),
        (hs.at[4:6, UP:inner], hs.at[0:2, UP:inner]),
        (hs.at[4:6, 0:UP], hs.at[0:2, 0:UP]),
        (hs.at[4:6, inner:], hs.at[0:2, inner:]),
        (share, passed),
    ]
    kinds = kinds + 4 * [kinds[2]]

    def remote(k):
        return pltpu.make_async_remote_copy(
            src_ref=routes[k][0],
            dst_ref=routes[k][1],
            send_sem=send_sem.at[k],
            recv_sem=recv_sem.at[k],
            device_id=kinds[k][0],
            device_id_type=MESH,
        )

    def send(k):
        @pl.when(kinds[k][1])
        def _():
            remote(k).start()

    def sent(k):
        @pl.when(kinds[k][1])
        def _():
            remote(k).wait_send()

    def arrived(k):
        @pl.when(kinds[k][2])
        def _():
            remote(k).wait_recv()

    for k in range(5):
        send(k)

    load_b = paired(wb_hbm, wb) + [load(bb_hbm, bb)]
    load_d = [
        load(wd_hbm.at[:, :, w], wd.at[:, :, :, w * chans : (w + 1) * chans]) for w in range(3)
    ] + [load(bd_hbm, bd)]
    blank(wb)

    @pl.when(first_s)
    def _():
        for field in (xs, hs):
            field[0:2] = jnp.zeros((2,) + field.shape[1:], BF16)
        passed[...] = jnp.zeros(passed.shape, F32)

    @pl.when(first_r)
    def _():
        xs[:, 0:UP] = jnp.zeros((6, UP, cols, chans), BF16)

    @pl.when(last_r)
    def _():
        xs[:, UP + height :] = jnp.zeros((6, LOW, cols, chans), BF16)

    def waited(copies):
        for copy in copies:
            copy.wait()

    def shifted(y0, y1, y2):
        n, width = y1.shape
        col = lax.broadcasted_iota(jnp.int32, (n // cols, cols, width), 1).reshape(n, width)
        left = jnp.where(col == 0, 0.0, pltpu.roll(y0, 1, 0))
        right = jnp.where(col == cols - 1, 0.0, pltpu.roll(y2, n - 1, 0))
        return y1 + left + right

    def stacked(field, frame, parts):
        got = [field[frame, lo:hi].reshape((hi - lo) * cols, chans) for lo, hi in parts]
        return got[0] if len(got) == 1 else jnp.concatenate(got, axis=0)

    def conv_pair(field, base, parts, weight):
        lhs = jnp.concatenate(
            [
                stacked(field, base + f, [(lo + h, hi + h) for lo, hi in parts])
                for f in range(4)
                for h in range(3)
            ],
            axis=1,
        )
        y = [
            jnp.dot(
                lhs,
                weight[:, :, w].reshape(12 * chans, 2 * chans),
                preferred_element_type=F32,
            )
            for w in range(3)
        ]
        return shifted(*y)

    def hidden_pair(base, parts):
        y = conv_pair(xs, base, parts, wa)
        for o in range(2):
            v = y[:, o * chans : (o + 1) * chans] + ba[...].reshape(1, chans)
            v = (v / (1.0 + jnp.exp(-v))).astype(BF16)
            at = 0
            for lo, hi in parts:
                n = (hi - lo) * cols
                hs[base + 2 + o, lo:hi] = v[at : at + n].reshape(hi - lo, cols, chans)
                at += n

    def hidden_rim(base):
        @pl.when(first_r)
        def _():
            hs[base + 2 : base + 4, 0 : UP - 1] = jnp.zeros((2, UP - 1, cols, chans), BF16)

        @pl.when(last_r)
        def _():
            hs[base + 2 : base + 4, hid_rows - 1 :] = jnp.zeros((2, 1, cols, chans), BF16)

    def mixed_pair(base):
        y = conv_pair(hs, base, [(0, mix_rows)], wb)
        for o in range(2):
            v = y[:, o * chans : (o + 1) * chans] + bb[...].reshape(1, chans)
            x = xs[base + 2 + o, UP - 1 : UP - 1 + mix_rows].reshape(mix_rows * cols, chans)
            v = x.astype(F32) + v
            ms[base + o] = v.astype(BF16).reshape(mix_rows, cols, chans)

        @pl.when(first_r)
        def _():
            ms[base : base + 2, 0:1] = jnp.zeros((2, 1, cols, chans), BF16)

    high = height // 2

    def down(base, first, count):
        lhs = jnp.concatenate(
            [
                jnp.concatenate([ms[base + t, 2 * q + h] for q in range(high)], axis=0)
                for t in range(count)
                for h in range(3)
            ],
            axis=1,
        )
        y = jnp.dot(
            lhs,
            wd[first : first + count].reshape(3 * count * chans, 3 * chans),
            preferred_element_type=F32,
        )
        return shifted(*[y[:, w * chans : (w + 1) * chans] for w in range(3)])

    def emit(j, extra):
        for i in range(high // 2):
            got = []
            for a in range(2):
                for b in range(2):
                    row = 2 * i + a
                    v = cells[j, pl.ds(row * cols + 2 * b, cols // 4, stride=4), :]
                    if extra is not None:
                        late = passed[pl.ds(row * (cols // 2) + b, cols // 4, stride=2), :]
                        v = v + late * extra
                    got.append(v)
            out[0, j, i] = jnp.concatenate(got, axis=1).astype(BF16)

    waited(load_x)
    waited(load_a)
    hidden_pair(2, [(UP, inner)])
    send(5)
    arrived(0)
    arrived(1)
    hidden_pair(2, [(0, UP), (inner, hid_rows)])
    hidden_rim(2)
    send(6)
    send(7)

    waited(load_i)
    start = jnp.int32(0)
    keep = jnp.int32(1)
    for i in range(lengths.shape[0]):
        keep = jnp.where(start == s, 0, keep)
        start = start + lengths[order[i]]
    keep = keep.astype(F32)

    def gate(field):
        block = field[0:2]
        field[0:2] = (block.astype(F32) * keep).astype(BF16)

    for k in (2, 3, 4):
        arrived(k)
    gate(xs)
    hidden_pair(0, [(0, hid_rows)])
    hidden_rim(0)
    waited(load_b)
    mixed_pair(2)
    waited(load_d)
    cells[0] = down(2, 0, 2)
    share[...] = cells[0, pl.ds(0, high * cols // 2, stride=2), :]
    send(8)
    for k in (5, 6, 7):
        arrived(k)
    gate(hs)
    mixed_pair(0)
    bias = bd[...].reshape(1, chans)
    cells[1] = down(0, 0, 3) + bias
    emit(1, None)
    cells[0] = down(0, 2, 1) + bias
    arrived(8)
    emit(0, keep)
    for k in range(9):
        sent(k)


def per_device(spans, rows_n, features, lengths, order, wa, ba, wb, bb, wd, bd):
    _, frames, height, cols, chans = features.shape
    hbm = pl.BlockSpec(memory_space=pltpu.HBM)
    vmem = pl.BlockSpec(memory_space=pltpu.VMEM)
    shape = (1, frames // 2, height // 4, cols // 4, 4 * chans)
    return pl.pallas_call(
        functools.partial(kernel, spans, rows_n),
        out_shape=jax.ShapeDtypeStruct(shape, BF16),
        in_specs=[hbm] * 9,
        out_specs=vmem,
        scratch_shapes=[
            pltpu.VMEM((frames + 2, height + UP + LOW, cols, chans), BF16),
            pltpu.VMEM((frames + 2, height + UP, cols, chans), BF16),
            pltpu.VMEM((frames, height + 1, cols, chans), BF16),
            pltpu.VMEM((4, 3, 3, chans, 2 * chans), BF16),
            pltpu.VMEM((4, 3, 3, chans, 2 * chans), BF16),
            pltpu.VMEM((3, 3, chans, 3 * chans), BF16),
            pltpu.VMEM((chans,), F32),
            pltpu.VMEM((chans,), F32),
            pltpu.VMEM((chans,), F32),
            pltpu.SMEM(lengths.shape, jnp.int32),
            pltpu.SMEM(order.shape, jnp.int32),
            pltpu.VMEM((2, height // 2 * cols, chans), F32),
            pltpu.VMEM((height // 4 * cols, chans), F32),
            pltpu.VMEM((height // 4 * cols, chans), F32),
            pltpu.SemaphoreType.DMA((9,)),
            pltpu.SemaphoreType.DMA((9,)),
            pltpu.SemaphoreType.DMA((22,)),
        ],
        compiler_params=pltpu.CompilerParams(
            collective_id=0, has_side_effects=True, vmem_limit_bytes=64 * 1024 * 1024
        ),
    )(features, lengths, order, wa, ba, wb, bb, wd, bd)


def solution(mesh):
    placed = (P("span", None, "row", None, None), P(), P(), P(), P(), P(), P(), P(), P())
    return jax.shard_map(
        functools.partial(per_device, mesh.shape["span"], mesh.shape["row"]),
        mesh=mesh,
        in_specs=placed,
        out_specs=P("span", None, "row", None, None),
        check_vma=False,
    )
```

profile of v0, /device:TPU:28, one launch (start us, length us, event | category | flops | bytes accessed | tf_op | source)
XLA Modules:
  0.0 15.0 jit_solution(16351969303467393466)
XLA Ops:
  0.0 13.6 %shard_map.91 = bf16[1,2,2,8,512]{4,3,2,1,0:T(8,128)(2,1)} custom-call(bf16[1,4,8,32,128]{4,3,2,1,0:T(8,128)(2,1)} %x_hbm.1, s32[4]{0:T(128)} %lengths_hbm.1, s32[4]{0:T(128)} %order_hbm.1, bf16[3,3,3,128,128]{4,3,2,1,0:T(8,128)(2,1)} %wa_hbm.1, f32[128]{0:T(128)} %ba_hbm.1, bf16[3,3,3,128,128]{4,3,2,1,0:T(8,128)(2,1)} %wb_hbm.1, f32[128]{0:T(128)} %bb_hbm.1, ...), custom_call_target="tpu_custom_call" | custom-call | tf_op jit(solution)/shard_map/pallas_call | solution.py:331
  13.6 1.4 %copy.11 = bf16[1,2,2,8,512]{4,3,2,1,0:T(8,128)(2,1)} copy(bf16[1,2,2,8,512]{4,3,2,1,0:T(8,128)(2,1)} %shard_map.91) | data formatting | bytes 65536
where the time goes:
time: 15.2 us; the launch traced here: 15 us
  Pallas kernels  13.6 us (89%)
  local copies, waits for them, and re-layouts  1.38 us (9%)
    pallas_call x1, Pallas kernels, per_device(): pl.pallas_call(functools.partial(kernel, spans, rows_n), out_shape=jax.Sh...  13.6 us
    unnamed x1, local copies, waits for them, and re-layouts  1.38 us

commit v1 on v0

--- a/solution.py
+++ b/solution.py
@@ -10,6 +10,7 @@
 MESH = pl.DeviceIdType.MESH
 UP = 3
 LOW = 2
+GROUP = 3
 BF16 = jnp.bfloat16
 F32 = jnp.float32
 
@@ -125,7 +126,7 @@
         (feats.at[2:4, 0:LOW], xs.at[0:2, UP + height : UP + height + LOW]),
         (hs.at[4:6, UP:inner], hs.at[0:2, UP:inner]),
         (hs.at[4:6, 0:UP], hs.at[0:2, 0:UP]),
-        (hs.at[4:6, inner:], hs.at[0:2, inner:]),
+        (hs.at[4:6, inner:hid_rows], hs.at[0:2, inner:hid_rows]),
         (share, passed),
     ]
     kinds = kinds + 4 * [kinds[2]]
@@ -176,7 +177,10 @@
 
     @pl.when(last_r)
     def _():
-        xs[:, UP + height :] = jnp.zeros((6, LOW, cols, chans), BF16)
+        xs[:, UP + height : UP + height + LOW] = jnp.zeros((6, LOW, cols, chans), BF16)
+
+    spare = xs.shape[1] - (UP + height + LOW)
+    xs[:, UP + height + LOW :] = jnp.zeros((6, spare, cols, chans), BF16)
 
     def waited(copies):
         for copy in copies:
@@ -190,13 +194,13 @@
         return y1 + left + right
 
     def stacked(field, frame, parts):
-        got = [field[frame, lo:hi].reshape((hi - lo) * cols, chans) for lo, hi in parts]
+        got = [field[frame, pl.ds(lo, n)].reshape(n * cols, chans) for lo, n in parts]
         return got[0] if len(got) == 1 else jnp.concatenate(got, axis=0)
 
     def conv_pair(field, base, parts, weight):
         lhs = jnp.concatenate(
             [
-                stacked(field, base + f, [(lo + h, hi + h) for lo, hi in parts])
+                stacked(field, base + f, [(lo + h, n) for lo, n in parts])
                 for f in range(4)
                 for h in range(3)
             ],
@@ -218,10 +222,9 @@
             v = y[:, o * chans : (o + 1) * chans] + ba[...].reshape(1, chans)
             v = (v / (1.0 + jnp.exp(-v))).astype(BF16)
             at = 0
-            for lo, hi in parts:
-                n = (hi - lo) * cols
-                hs[base + 2 + o, lo:hi] = v[at : at + n].reshape(hi - lo, cols, chans)
-                at += n
+            for lo, n in parts:
+                hs[base + 2 + o, pl.ds(lo, n)] = v[at : at + n * cols].reshape(n, cols, chans)
+                at += n * cols
 
     def hidden_rim(base):
         @pl.when(first_r)
@@ -230,7 +233,7 @@
 
         @pl.when(last_r)
         def _():
-            hs[base + 2 : base + 4, hid_rows - 1 :] = jnp.zeros((2, 1, cols, chans), BF16)
+            hs[base + 2 : base + 4, hid_rows - 1 : hid_rows] = jnp.zeros((2, 1, cols, chans), BF16)
 
     def mixed_pair(base):
         y = conv_pair(hs, base, [(0, mix_rows)], wb)
@@ -242,7 +245,8 @@
 
         @pl.when(first_r)
         def _():
-            ms[base : base + 2, 0:1] = jnp.zeros((2, 1, cols, chans), BF16)
+            for o in range(2):
+                ms[base + o, 0:1] = jnp.zeros((1, cols, chans), BF16)
 
     high = height // 2
 
@@ -273,19 +277,10 @@
                         late = passed[pl.ds(row * (cols // 2) + b, cols // 4, stride=2), :]
                         v = v + late * extra
                     got.append(v)
-            out[0, j, i] = jnp.concatenate(got, axis=1).astype(BF16)
+            out[0, j, i] = jnp.concatenate(got, axis=1)
 
     waited(load_x)
     waited(load_a)
-    hidden_pair(2, [(UP, inner)])
-    send(5)
-    arrived(0)
-    arrived(1)
-    hidden_pair(2, [(0, UP), (inner, hid_rows)])
-    hidden_rim(2)
-    send(6)
-    send(7)
-
     waited(load_i)
     start = jnp.int32(0)
     keep = jnp.int32(1)
@@ -298,21 +293,57 @@
         block = field[0:2]
         field[0:2] = (block.astype(F32) * keep).astype(BF16)
 
-    for k in (2, 3, 4):
-        arrived(k)
-    gate(xs)
-    hidden_pair(0, [(0, hid_rows)])
-    hidden_rim(0)
+    @pl.loop(0, 4)
+    def _(i):
+        @pl.when(i == 1)
+        def _():
+            arrived(0)
+            arrived(1)
+
+        @pl.when(i == 2)
+        def _():
+            for k in (2, 3, 4):
+                arrived(k)
+            gate(xs)
+
+        outer = i % 2
+        low = UP - GROUP * outer
+        up = UP + GROUP + GROUP * outer
+        hidden_pair(2 - 2 * (i // 2), [(low, GROUP), (up, GROUP)])
+
+        @pl.when(i == 0)
+        def _():
+            send(5)
+
+        @pl.when(i == 1)
+        def _():
+            hidden_rim(2)
+            send(6)
+            send(7)
+
+        @pl.when(i == 3)
+        def _():
+            hidden_rim(0)
+
     waited(load_b)
-    mixed_pair(2)
-    waited(load_d)
-    cells[0] = down(2, 0, 2)
-    share[...] = cells[0, pl.ds(0, high * cols // 2, stride=2), :]
-    send(8)
-    for k in (5, 6, 7):
-        arrived(k)
-    gate(hs)
-    mixed_pair(0)
+
+    @pl.loop(0, 2)
+    def _(i):
+        @pl.when(i == 1)
+        def _():
+            for k in (5, 6, 7):
+                arrived(k)
+            gate(hs)
+
+        mixed_pair(2 - 2 * i)
+
+        @pl.when(i == 0)
+        def _():
+            waited(load_d)
+            cells[0] = down(2, 0, 2)
+            share[...] = cells[0, pl.ds(0, high * cols // 2, stride=2), :]
+            send(8)
+
     bias = bd[...].reshape(1, chans)
     cells[1] = down(0, 0, 3) + bias
     emit(1, None)
@@ -330,12 +361,12 @@
     shape = (1, frames // 2, height // 4, cols // 4, 4 * chans)
     return pl.pallas_call(
         functools.partial(kernel, spans, rows_n),
-        out_shape=jax.ShapeDtypeStruct(shape, BF16),
+        out_shape=jax.ShapeDtypeStruct(shape, F32),
         in_specs=[hbm] * 9,
         out_specs=vmem,
         scratch_shapes=[
-            pltpu.VMEM((frames + 2, height + UP + LOW, cols, chans), BF16),
-            pltpu.VMEM((frames + 2, height + UP, cols, chans), BF16),
+            pltpu.VMEM((frames + 2, 4 * GROUP + 2, cols, chans), BF16),
+            pltpu.VMEM((frames + 2, 4 * GROUP, cols, chans), BF16),
             pltpu.VMEM((frames, height + 1, cols, chans), BF16),
             pltpu.VMEM((4, 3, 3, chans, 2 * chans), BF16),
             pltpu.VMEM((4, 3, 3, chans, 2 * chans), BF16),
@@ -355,7 +386,7 @@
         compiler_params=pltpu.CompilerParams(
             collective_id=0, has_side_effects=True, vmem_limit_bytes=64 * 1024 * 1024
         ),
-    )(features, lengths, order, wa, ba, wb, bb, wd, bd)
+    )(features, lengths, order, wa, ba, wb, bb, wd, bd).astype(BF16)
 
 
 def solution(mesh):

time: 15.2 us -> 15.1 us (level)
  other arithmetic: 0 us -> 1.46 us
  local copies, waits for them, and re-layouts: 1.38 us -> 0 us
    convert_element_type x0 -> x1, other arithmetic: none -> 1.46 us  [per_device(): return pl.pallas_call(functools.partial(kernel, spans, rows_n), out_shape...]
    unnamed x1 -> x0, local copies, waits for them, and re-layouts: 1.38 us -> none
where the time goes in v1:
time: 15.1 us; the launch traced here: 14.9 us
  Pallas kernels  13.5 us (89%)
  other arithmetic  1.46 us (10%)
    pallas_call x1, Pallas kernels, per_device(): pl.pallas_call(functools.partial(kernel, spans, rows_n), out_shape=jax.Sh...  13.5 us
    convert_element_type x1, other arithmetic, per_device(): return pl.pallas_call(functools.partial(kernel, spans, rows_n), out_shape...  1.46 us

profile of v1, /device:TPU:28, one launch (start us, length us, event | category | flops | bytes accessed | tf_op | source)
XLA Modules:
  0.0 14.9 jit_solution(16221308460597412224)
XLA Ops:
  0.0 13.5 %shard_map.91 = f32[1,2,2,8,512]{4,3,2,1,0:T(8,128)} custom-call(bf16[1,4,8,32,128]{4,3,2,1,0:T(8,128)(2,1)} %x_hbm.1, s32[4]{0:T(128)} %lengths_hbm.1, s32[4]{0:T(128)} %order_hbm.1, bf16[3,3,3,128,128]{4,3,2,1,0:T(8,128)(2,1)} %wa_hbm.1, f32[128]{0:T(128)} %ba_hbm.1, bf16[3,3,3,128,128]{4,3,2,1,0:T(8,128)(2,1)} %wb_hbm.1, f32[128]{0:T(128)} %bb_hbm.1, ...), custom_call_target="tpu_custom_call" | custom-call | tf_op jit(solution)/shard_map/pallas_call | solution.py:362
  13.5 1.5 %convert_element_type.3 = bf16[1,2,2,8,512]{4,3,2,1,0:T(8,128)(2,1)} convert(f32[1,2,2,8,512]{4,3,2,1,0:T(8,128)} %shard_map.91) | non-fusion elementwise | flops 16384 | bytes 98304 | tf_op jit(solution)/shard_map/convert_element_type | solution.py:389
